TPU v7x, 768 devices: a whole 4x8x12 slice. The times are simulated.
768 devices in a mesh: fsdp: 32 (over x, y_lo, core), rep: 24 (over z, y_hi).
Axes of the slice: x: 4, y: 8 (y_hi: 2, y_lo: 4; y = y_hi * 4 + y_lo), z: 12, core: 2. Of those that a mesh axis runs over, the one named last changes fastest.
Arguments:
- tokens: bfloat16 [4096, 24, 8192], P('fsdp', 'rep'), may hold values from -30 to 30
- norm_gain: float32 [8192], replicated, may hold values from 0.5 to 2
- w_value: bfloat16 [8192, 512], P('fsdp'), may hold values from -0.25 to 0.25
- grad_value: bfloat16 [4096, 24, 512], P('fsdp', 'rep'), may hold values from -6 to 6
Outputs:
- dw_value: float32 [8192, 512], P('fsdp')
- dtokens: bfloat16 [4096, 24, 8192], P(None, 'rep', 'fsdp')
All inputs are finite; a program needn't handle non-finite values.
Results may differ from a plain program's by a relative error of at most 0.0029.
Values may be sent and summed in bfloat16 or wider, within the bound.
A program may use at most 32 MiB of HBM per device.

v0:
```python
import jax
import jax.numpy as jnp
from jax import lax
from jax.sharding import PartitionSpec as P

D = 8192


def body(tokens, norm_gain, w_value, grad_value):
    local_width = w_value.shape[0]
    offset = lax.axis_index("fsdp") * local_width
    own_gain = lax.dynamic_slice_in_dim(norm_gain, offset, local_width, 0)
    flat_tokens = tokens[:, 0, :]
    flat_grads = grad_value[:, 0, :]
    columns = lax.all_to_all(flat_tokens, "fsdp", split_axis=1, concat_axis=0, tiled=True)
    values = columns.astype(jnp.float32)
    squares = lax.psum(jnp.sum(values * values, axis=1), "fsdp")
    scale = lax.rsqrt(squares / D + 1e-05)[:, None]
    normed = (values * scale * own_gain).astype(jnp.bfloat16)
    contract = (((0,), (0,)), ((), ()))
    back = (((1,), (1,)), ((), ()))
    all_grads = lax.all_gather(flat_grads, "fsdp", axis=0, tiled=True)
    weight_part = lax.dot_general(normed, all_grads, contract, preferred_element_type=jnp.float32)
    dnormed = lax.dot_general(all_grads, w_value, back, preferred_element_type=jnp.float32)
    inner = lax.psum(jnp.sum(values * own_gain * dnormed, axis=1), "fsdp")[:, None]
    dvalues = scale * own_gain * dnormed - values * scale * scale * scale * inner / D
    dtokens = dvalues.astype(jnp.bfloat16)[:, None, :]
    dw_value = lax.psum(weight_part, "rep")
    return (dw_value, dtokens)


def solution(mesh):
    in_specs = (P("fsdp", "rep", None), P(), P("fsdp", None), P("fsdp", "rep", None))
    out_specs = (P("fsdp", None), P(None, "rep", "fsdp"))
    return jax.shard_map(body, mesh=mesh, in_specs=in_specs, out_specs=out_specs, check_vma=False)
```

profile of v0, /device:TPU:2, one launch (start us, length us, event | category | flops | bytes accessed | tf_op | source)
XLA Modules:
  0.0 550.4 jit_solution(14519858036701515635)
XLA Ops:
  7.2 0.0 copy-start
  7.2 0.0 all-gather.3.cloned.1.call-start
  7.2 0.7 all-gather.3.cloned.1.call-update
  7.9 4.1 copy.10
  12.0 13.3 %all-to-all-start = ((bf16[128,32,256]{0,2,1:T(8,128)(2,1)}), bf16[128,32,256]{0,2,1:T(8,128)(2,1)S(1)}, u32[]{:S(2)}, u32[]{:S(2)}) async-start(bf16[128,32,256]{0,2,1:T(8,128)(2,1)} %bitcast.35), calls=%async_computation | async-start | bytes 4194304 | tf_op jit(solution)/shard_map/all_to_all | solution.py:15
  25.3 0.0 all-reduce.3.cloned.1.call-start
  25.3 0.8 dynamic_slice.3
  26.1 63.5 %all-to-all-done = bf16[128,32,256]{0,2,1:T(8,128)(2,1)S(1)} async-done(((bf16[128,32,256]{0,2,1:T(8,128)(2,1)}), bf16[128,32,256]{0,2,1:T(8,128)(2,1)S(1)}, u32[]{:S(2)}, u32[]{:S(2)}) %all-to-all-start) | async-done | bytes 2097184 | tf_op jit(solution)/shard_map/all_to_all | solution.py:15
  89.6 0.4 fusion
  90.0 13.8 %all-gather.3.cloned.1.call-done = bf16[4096,1,512]{2,0,1:T(8,128)(2,1)} async-done(((bf16[128,1,512]{2,0,1:T(8,128)(2,1)}), bf16[4096,1,512]{2,0,1:T(8,128)(2,1)}) %all-gather.3.cloned.1.call-update) | async-done | bytes 4194320 | tf_op jit(solution)/shard_map/all_gather | solution.py:22
  103.8 0.0 copy-done
  103.8 5.4 fusion.2
  109.2 116.8 %all-reduce = (f32[4096]{0:T(1024)S(1)}, f32[4096]{0:T(1024)S(1)}) all-reduce(f32[4096]{0:T(1024)S(1)} %bitcast.36, f32[4096]{0:T(1024)S(1)} %get-tuple-element.10), channel_id=1, replica_groups=mesh['fsdp'=32,'rep'=24] {'fsdp'}, use_global_device_ids=true, to_apply=%region_1.0 | all-reduce | flops 8192 | bytes 65536 | tf_op jit(solution)/shard_map/psum | solution.py:17
  226.1 4.3 fusion.5
  230.3 0.0 all-reduce.3.cloned.1.call-update
  230.4 4.8 fusion.9
  235.2 4.1 copy.12
  239.2 302.5 %all-reduce.3.cloned.1.call-done = f32[256,512]{1,0:T(8,128)} async-done(((f32[256,512]{1,0:T(8,128)}), f32[256,512]{1,0:T(8,128)}) %all-reduce.3.cloned.1.call-update) | async-done | bytes 524304 | tf_op jit(solution)/shard_map/psum | solution.py:28
  541.7 1.9 copy.21
  (1 shorter events, 0.0 us)
Async XLA Ops:
  7.2 96.7 %copy-start = (bf16[256,512]{1,0:T(8,128)(2,1)S(1)}, bf16[256,512]{1,0:T(8,128)(2,1)}, u32[]{:S(2)}) copy-start(bf16[256,512]{1,0:T(8,128)(2,1)} %param.6) | copy-start | bytes 786436
  7.2 96.6 %all-gather.3.cloned.1.call-start = ((), (), s32[]{:S(2)}) async-start(), calls=%async_computation.2 | async-start | bytes 4325376 | tf_op jit(solution)/shard_map/all_gather | solution.py:22
  12.0 77.6 %all-to-all-start = ((bf16[128,32,256]{0,2,1:T(8,128)(2,1)}), bf16[128,32,256]{0,2,1:T(8,128)(2,1)S(1)}, u32[]{:S(2)}, u32[]{:S(2)}) async-start(bf16[128,32,256]{0,2,1:T(8,128)(2,1)} %bitcast.35), calls=%async_computation | async-start | bytes 4194304 | tf_op jit(solution)/shard_map/all_to_all | solution.py:15
  25.3 516.4 %all-reduce.3.cloned.1.call-start = ((), (), s32[]{:S(2)}) async-start(), calls=%async_computation.1 | async-start | bytes 1048576 | tf_op jit(solution)/shard_map/psum | solution.py:28
Sparse Core Ops, SparseCore 0:
  10.5 93.3 all-gather.2
  230.5 311.1 all-reduce.2
where the time goes:
time: 551 us; the launch traced here: 550 us
  waiting for transfers between devices  380 us (69%)
  blocking collectives  117 us (21%)
  between operations  14.1 us (3%)
  starting transfers between devices  13.3 us (2%)
  local copies, waits for them, and re-layouts  10.8 us (2%)
  matrix products  9.67 us (2%)
    psum x1, waiting for transfers between devices, body(): dw_value = lax.psum(weight_part, 'rep')  302 us
    psum x1, blocking collectives, body(): squares = lax.psum(jnp.sum(values * values, axis=1), 'fsdp')  117 us
    all_to_all x1, waiting for transfers between devices, body(): lax.all_to_all(flat_tokens, 'fsdp', split_axis=1, concat_axis=0, tiled=True)  63.5 us
    all_gather x1, waiting for transfers between devices, body(): all_grads = lax.all_gather(flat_grads, 'fsdp', axis=0, tiled=True)  13.8 us
    all_to_all x1, starting transfers between devices, body(): lax.all_to_all(flat_tokens, 'fsdp', split_axis=1, concat_axis=0, tiled=True)  13.3 us
  transfers between devices with their start and end apart: 3, of which 3 were waited for; matrix products, arithmetic and copies ran while one was open for 3% of the time, Pallas kernels for 0%

commit v1 on v0

v1 whole, which is shorter than its diff:
```python
import functools
import jax
import jax.numpy as jnp
from jax import lax
from jax.experimental import pallas as pl
from jax.experimental.pallas import tpu as pltpu
from jax.sharding import PartitionSpec as P

MESH = pl.DeviceIdType.MESH
NX, NY, NC = 4, 4, 2
NZ, NH = 12, 2
NF, NR = NX * NY * NC, NZ * NH
T = 128
F = 128
C = 512
D = 2 * F * NF
OWN = 8
PR = F // OWN
f32, bf16 = jnp.float32, jnp.bfloat16


def kernel(tok, gain, w, grd, dw, dt, vtok, tbuf, gbuf, dn, pacc, sc, colc, rows, acc, rsb, psum, prb, agb, dtb, dwb,
           lsem, gsend, grecv, tsend, trecv, ssem, rsem):
    me, rep = lax.axis_index("fsdp"), lax.axis_index("rep")
    x, y, c = me // (NY * NC), (me // NC) % NY, me % NC
    z, h = rep // NH, rep % NH

    def slot_of(x, y, c):
        return c * (NX * NY) + x * NY + y

    def slot_at(k):
        s = (me + NF - k) % NF
        return slot_of(s // (NY * NC), (s // NC) % NY, s % NC)

    mine = slot_of(x, y, c)
    owner = z % 3 < 2
    piece = (z // 3) * 2 + z % 3

    def local(src, dst, sem):
        return pltpu.make_async_copy(src, dst, sem)

    def to(src, dst, ss, rs, f, r):
        return pltpu.make_async_remote_copy(src_ref=src, dst_ref=dst, send_sem=ss, recv_sem=rs, device_id=(f, r), device_id_type=MESH)

    def wait(ref, sem):
        pltpu.make_async_copy(ref, ref, sem).wait()

    bar = pltpu.get_barrier_semaphore()

    def greet_f(k, _):
        pl.semaphore_signal(bar, inc=1, device_id=((me + k) % NF, rep), device_id_type=MESH)
        return 0

    def greet_z(k, _):
        pl.semaphore_signal(bar, inc=1, device_id=(me, (z + k) % NZ * NH + h), device_id_type=MESH)
        return 0

    lax.fori_loop(1, NF, greet_f, 0)
    lax.fori_loop(1, NZ, greet_z, 0)
    pl.semaphore_signal(bar, inc=1, device_id=(me, z * NH + 1 - h), device_id_type=MESH)

    load = local(tok, vtok, lsem.at[0])
    load.start()
    own_g = local(grd, gbuf.at[mine], lsem.at[1])
    own_g.start()
    own_t = [local(tok.at[:, pl.ds(pl.multiple_of((me * 2 + i) * F, F), F)], tbuf.at[i * NF + mine], trecv.at[i * NF + mine]) for i in range(2)]
    for cp in own_t:
        cp.start()
    load.wait()

    def square(i, a):
        v = vtok[:, pl.ds(pl.multiple_of(i * F, F), F)].astype(f32)
        return a + v * v

    total = lax.fori_loop(0, D // F, square, jnp.zeros((T, F), f32), unroll=4)
    srow = lax.rsqrt(jnp.sum(total.T, axis=0, keepdims=True) / D + 1e-05)
    sc[mine] = srow
    pl.semaphore_wait(bar, NF - 1 + NZ)

    own_g.wait()
    for j in range(1, NY):
        to(gbuf.at[mine], gbuf.at[mine], gsend.at[j - 1], grecv.at[mine], x * (NY * NC) + (y + j) % NY * NC + c, rep).start()
    for j in range(1, NX):
        to(gbuf.at[mine], gbuf.at[mine], gsend.at[NY + j - 2], grecv.at[mine], (x + j) % NX * (NY * NC) + y * NC + c, rep).start()
    to(gbuf.at[mine], gbuf.at[mine], gsend.at[NY + NX - 2], grecv.at[mine], me + 1 - 2 * c, rep).start()
    n_g = NY + NX - 1

    def send_scale(k, _):
        to(sc.at[mine], sc.at[mine], ssem.at[0], rsem.at[0], (me + k) % NF, rep).start()
        return 0

    lax.fori_loop(1, NF, send_scale, 0)

    def send_tokens(i):
        def body(k, _):
            d = (me + k) % NF
            to(tok.at[:, pl.ds(pl.multiple_of((d * 2 + i) * F, F), F)], tbuf.at[i * NF + mine], tsend.at[i], trecv.at[i * NF + mine], d, rep).start()
            return 0
        lax.fori_loop(1, NF, body, 0)

    send_tokens(0)
    for i in range(1, NY):
        s = slot_of(x, (y + i) % NY, c)
        wait(gbuf.at[s], grecv.at[s])
        for j in range(1, NX):
            to(gbuf.at[s], gbuf.at[s], gsend.at[n_g], grecv.at[s], (x + j) % NX * (NY * NC) + y * NC + c, rep).start()
            n_g += 1
        to(gbuf.at[s], gbuf.at[s], gsend.at[n_g], grecv.at[s], me + 1 - 2 * c, rep).start()
        n_g += 1
    send_tokens(1)

    def dnormed(s):
        dn[s] = lax.dot_general(gbuf[s], w[...], (((1,), (1,)), ((), ())), preferred_element_type=f32)

    for i in range(NY):
        for j in range(1, NX):
            s = slot_of((x + j) % NX, (y + i) % NY, c)
            wait(gbuf.at[s], grecv.at[s])
            to(gbuf.at[s], gbuf.at[s], gsend.at[n_g], grecv.at[s], me + 1 - 2 * c, rep).start()
            n_g += 1

    def near(i, _):
        dnormed(c * (NX * NY) + i)
        return 0

    def far(i, _):
        s = (1 - c) * (NX * NY) + i
        wait(gbuf.at[s], grecv.at[s])
        dnormed(s)
        return 0

    lax.fori_loop(0, NX * NY, near, 0)
    lax.fori_loop(0, NX * NY, far, 0)

    def columns(ref):
        flat = jnp.concatenate([ref[s] for s in range(NF)] + [jnp.zeros((T - NF, T), f32)], axis=0).T
        return flat

    wait(sc.at[pl.ds(0, NF - 1)], rsem.at[0])
    flat = columns(sc)
    for s in range(NF):
        colc[0, s] = flat[:, s:s + 1]

    def gains(i):
        return gain[pl.ds(me * 2 + i, 1), :]

    def block(i, k):
        s = slot_at(k)
        wait(tbuf.at[i * NF + s], trecv.at[i * NF + s])
        v = tbuf[i * NF + s].astype(f32)
        normed = (v * colc[0, s] * gains(i)).astype(bf16)
        part = lax.dot_general(normed, gbuf[s], (((0,), (0,)), ((), ())), preferred_element_type=f32)
        acc[i] += part
        p = v * gains(i) * dn[s, :, i * F:(i + 1) * F]
        return s, p

    acc[...] = jnp.zeros_like(acc)

    def first(k, _):
        s, p = block(0, k)
        pacc[s] = p
        return 0

    lax.fori_loop(0, NF, first, 0)

    def dw_scatter(i):
        for p in range(OWN):
            zo = p // 2 * 3 + p % 2

            @pl.when(z != zo)
            def _():
                to(acc.at[i, pl.ds(p * PR, PR)], rsb.at[i, z], ssem.at[3 + i], rsem.at[3 + i], me, zo * NH + h).start()

    def dw_pair(i):
        @pl.when(owner)
        def _():
            wait(rsb.at[i, pl.ds(0, NZ - 1)], rsem.at[3 + i])
            rsb[i, z] = acc[i, pl.ds(pl.multiple_of(piece * PR, PR), PR)]
            psum[i] = functools.reduce(jnp.add, [rsb[i, j] for j in range(NZ)])
            to(psum.at[i], prb.at[i], ssem.at[5 + i], rsem.at[5 + i], me, z * NH + 1 - h).start()

    def dw_gather(i):
        @pl.when(owner)
        def _():
            wait(prb.at[i], rsem.at[5 + i])
            agb[i, piece] = (psum[i] + prb[i]).astype(bf16)

            def body(k, _):
                to(agb.at[i, piece], agb.at[i, piece], ssem.at[7 + i], rsem.at[7 + i], me, (z + k) % NZ * NH + h).start()
                return 0
            lax.fori_loop(1, NZ, body, 0)

    def dw_finish(i):
        @pl.when(owner)
        def _():
            wait(agb.at[i, pl.ds(0, OWN - 1)], rsem.at[7 + i])

        @pl.when(jnp.logical_not(owner))
        def _():
            wait(agb.at[i, pl.ds(0, OWN)], rsem.at[7 + i])
        for p in range(OWN):
            dwb[pl.ds(i * F + p * PR, PR), :] = agb[i, p].astype(f32)
        local(dwb.at[pl.ds(i * F, F)], dw.at[pl.ds(i * F, F)], lsem.at[2 + i]).start()

    def second(k, _):
        s, p = block(1, k)
        rows[0, s] = jnp.sum((p + pacc[s]).T, axis=0, keepdims=True)

        @pl.when(k > 0)
        def _():
            to(rows.at[0, s], rows.at[1, mine], ssem.at[1], rsem.at[1], (me + NF - k) % NF, rep).start()
        return 0

    dw_scatter(0)
    lax.fori_loop(0, NF // 2, second, 0)
    dw_pair(0)
    lax.fori_loop(NF // 2, NF * 3 // 4, second, 0)
    dw_gather(0)
    lax.fori_loop(NF * 3 // 4, NF, second, 0)
    dw_scatter(1)

    wait(rows.at[1, pl.ds(0, NF - 1)], rsem.at[1])
    rows[1, mine] = rows[0, mine]
    inner = functools.reduce(jnp.add, [rows[1, s] for s in range(NF)])
    srow = sc[mine]
    rows[2, mine] = srow * srow * srow * inner / D

    def send_coef(k, _):
        to(rows.at[2, mine], rows.at[2, mine], ssem.at[2], rsem.at[2], (me + k) % NF, rep).start()
        return 0

    lax.fori_loop(1, NF, send_coef, 0)
    dw_finish(0)
    dw_pair(1)
    wait(rows.at[2, pl.ds(0, NF - 1)], rsem.at[2])
    flat = columns(rows.at[2])
    for s in range(NF):
        colc[1, s] = flat[:, s:s + 1]

    def finish(k, _):
        xs = k // (NY * NC)
        s = slot_of(xs, (k // NC) % NY, k % NC)
        for i in range(2):
            a = colc[0, s] * gains(i) * dn[s, :, i * F:(i + 1) * F]
            dtb[k, :, i * F:(i + 1) * F] = (a - tbuf[i * NF + s].astype(f32) * colc[1, s]).astype(bf16)
        local(dtb.at[k], dt.at[pl.ds(pl.multiple_of(k * T, T), T)], lsem.at[4]).start()
        return 0

    lax.fori_loop(0, NF, finish, 0)
    dw_gather(1)
    dw_finish(1)

    for i in range(2):
        wait(tbuf.at[pl.ds(0, NF - 1)], tsend.at[i])
        wait(dwb.at[pl.ds(i * F, F)], lsem.at[2 + i])

        @pl.when(owner)
        def _():
            wait(acc.at[i, pl.ds(0, F - PR)], ssem.at[3 + i])
            wait(psum.at[i], ssem.at[5 + i])
            wait(agb.at[pl.ds(0, 1)].at[0, pl.ds(0, OWN)], ssem.at[7 + i])
            wait(agb.at[0, pl.ds(0, NZ - 1 - OWN)], ssem.at[7 + i])

        @pl.when(jnp.logical_not(owner))
        def _():
            wait(acc.at[i], ssem.at[3 + i])
    for i in range(3):
        wait(rows.at[0, pl.ds(0, NF - 1)], ssem.at[i])
    for j in range(n_g):
        wait(gbuf.at[0], gsend.at[j])
    wait(dtb, lsem.at[4])


def body(tokens, norm_gain, w_value, grad_value):
    anyspace, vmem = pl.BlockSpec(memory_space=pl.ANY), pl.BlockSpec(memory_space=pltpu.VMEM)
    dma = pltpu.SemaphoreType.DMA
    dw, dt = pl.pallas_call(
        kernel,
        out_shape=(jax.ShapeDtypeStruct((2 * F, C), f32), jax.ShapeDtypeStruct((NF * T, 2 * F), bf16)),
        in_specs=[anyspace, vmem, vmem, anyspace],
        out_specs=(anyspace, anyspace),
        scratch_shapes=[
            pltpu.VMEM((T, D), bf16),
            pltpu.VMEM((2 * NF, T, F), bf16),
            pltpu.VMEM((NF, T, C), bf16),
            pltpu.VMEM((NF, T, 2 * F), f32),
            pltpu.VMEM((NF, T, F), f32),
            pltpu.VMEM((NF, 1, T), f32),
            pltpu.VMEM((2, NF, T, 1), f32),
            pltpu.VMEM((3, NF, 1, T), f32),
            pltpu.VMEM((2, F, C), f32),
            pltpu.VMEM((2, NZ, PR, C), f32),
            pltpu.VMEM((2, PR, C), f32),
            pltpu.VMEM((2, PR, C), f32),
            pltpu.VMEM((2, OWN, PR, C), bf16),
            pltpu.VMEM((NF, T, 2 * F), bf16),
            pltpu.VMEM((2 * F, C), f32),
            dma((5,)), dma((48,)), dma((NF,)), dma((2,)), dma((2 * NF,)), dma((9,)), dma((9,)),
        ],
        compiler_params=pltpu.CompilerParams(collective_id=0, has_side_effects=True, vmem_limit_bytes=48 << 20),
    )(tokens.reshape(T, D), norm_gain.reshape(2 * NF, F), w_value, grad_value.reshape(T, C))
    return dw, dt.reshape(NF * T, 1, 2 * F)


def solution(mesh):
    assert mesh.shape["fsdp"] == NF and mesh.shape["rep"] == NR
    in_specs = (P("fsdp", "rep", None), P(), P("fsdp", None), P("fsdp", "rep", None))
    out_specs = (P("fsdp", None), P(None, "rep", "fsdp"))
    return jax.shard_map(body, mesh=mesh, in_specs=in_specs, out_specs=out_specs, check_vma=False)
```

time: 551 us -> 140 us (0.25)
  the two profiles are of different devices: /device:TPU:2 before, /device:TPU:14 now
where the time goes in v1:
time: 140 us
  Pallas kernels  133 us (95%)
  local copies, waits for them, and re-layouts  6.31 us (5%)
    pallas_call x1, Pallas kernels, body(): pl.pallas_call(kernel, out_shape=(jax.ShapeDtypeStruct((2 * F, C), f32),...  133 us
    unnamed x10, local copies, waits for them, and re-layouts  6.31 us

profile of v1, /device:TPU:14, one launch (start us, length us, event | category | flops | bytes accessed | tf_op | source)
XLA Modules:
  0.0 140.0 jit_solution(13350037126970086674)
XLA Ops:
  0.6 0.0 copy-start
  0.6 1.6 %copy-done = bf16[128,1,8192]{2,0,1:T(8,128)(2,1)S(1)} copy-done((bf16[128,1,8192]{2,0,1:T(8,128)(2,1)S(1)}, bf16[128,1,8192]{2,0,1:T(8,128)(2,1)}, u32[]{:S(2)}) %copy-start) | copy-done | bytes 2097176
  2.2 0.0 copy-start.1
  2.2 0.9 copy-done.1
  3.2 0.0 copy-start.2
  3.2 0.9 copy-done.2
  4.1 0.0 copy-start.3
  4.1 0.8 copy-done.3
  4.8 133.0 %shard_map.59 = (f32[256,512]{1,0:T(8,128)S(1)}, bf16[4096,256]{1,0:T(8,128)(2,1)S(1)}) custom-call(bf16[128,8192]{1,0:T(8,128)(2,1)S(1)} %bitcast.4, f32[64,128]{1,0:T(8,128)S(1)} %bitcast.7, bf16[256,512]{1,0:T(8,128)(2,1)S(1)} %copy-done.1, bf16[128,512]{1,0:T(8,128)(2,1)S(1)} %bitcast.6), custom_call_target="tpu_custom_call" | custom-call | tf_op jit(solution)/shard_map/pallas_call | solution.py:277
  137.8 0.8 copy.8
  138.6 1.3 copy.9
Async XLA Ops:
  0.6 1.6 %copy-start = (bf16[128,1,8192]{2,0,1:T(8,128)(2,1)S(1)}, bf16[128,1,8192]{2,0,1:T(8,128)(2,1)}, u32[]{:S(2)}) copy-start(bf16[128,1,8192]{2,0,1:T(8,128)(2,1)} %param.4) | copy-start | bytes 6291460
  2.2 0.9 copy-start.1
  3.2 0.9 copy-start.2
  4.1 0.8 copy-start.3

commit v2 on v1

v2 whole, which is shorter than its diff:
```python
import functools
import jax
import jax.numpy as jnp
from jax import lax
from jax.experimental import pallas as pl
from jax.experimental.pallas import tpu as pltpu
from jax.sharding import PartitionSpec as P

MESH = pl.DeviceIdType.MESH
NX, NY, NC = 4, 4, 2
NZ, NH = 12, 2
NF, NR = NX * NY * NC, NZ * NH
T = 128
F = 128
C = 512
D = 2 * F * NF
OWN = 8
PR = F // OWN
L = NY
NG = NF // L
f32, bf16 = jnp.float32, jnp.bfloat16


def kernel(tok, gain, w, grd, dw, dt, vtok, tbuf, gbuf, dn, pacc, sc, colc, rows, acc, accb, rsf, rsb, psum, prb, agb, dtb, dwb,
           lsem, gsend, csend, grecv, tsend, trecv, ssem, rsem):
    me, rep = lax.axis_index("fsdp"), lax.axis_index("rep")
    x, y, c = me // (NY * NC), (me // NC) % NY, me % NC
    z, h = rep // NH, rep % NH

    def slot_of(x, y, c):
        return c * (NX * NY) + x * NY + y

    def shift(q):
        r = q % NX
        return r + r // 2 * (1 - 2 * (r % 2)), q // NX

    def base_of(q):
        dx, dc = shift(q)
        return slot_of((x + NX - dx) % NX, 0, (c + dc) % NC)

    mine = slot_of(x, y, c)
    owner = z % 3 < 2
    piece = (z // 3) * 2 + z % 3

    def local(src, dst, sem):
        return pltpu.make_async_copy(src, dst, sem)

    def to(src, dst, ss, rs, f, r):
        return pltpu.make_async_remote_copy(src_ref=src, dst_ref=dst, send_sem=ss, recv_sem=rs, device_id=(f, r), device_id_type=MESH)

    def wait(ref, sem):
        pltpu.make_async_copy(ref, ref, sem).wait()

    bar = pltpu.get_barrier_semaphore()

    def greet_f(k, _):
        pl.semaphore_signal(bar, inc=1, device_id=((me + k) % NF, rep), device_id_type=MESH)
        return 0

    def greet_z(k, _):
        pl.semaphore_signal(bar, inc=1, device_id=(me, (z + k) % NZ * NH + h), device_id_type=MESH)
        return 0

    lax.fori_loop(1, NF, greet_f, 0)
    lax.fori_loop(1, NZ, greet_z, 0)
    pl.semaphore_signal(bar, inc=1, device_id=(me, z * NH + 1 - h), device_id_type=MESH)

    load = local(tok, vtok, lsem.at[0])
    load.start()
    own_g = local(grd, gbuf.at[mine], lsem.at[1])
    own_g.start()
    own_t = [local(tok.at[:, pl.ds(pl.multiple_of((me * 2 + i) * F, F), F)], tbuf.at[i * NF + mine], trecv.at[i * NF + mine]) for i in range(2)]
    for cp in own_t:
        cp.start()
    load.wait()

    def square(i, a):
        v = vtok[:, pl.ds(pl.multiple_of(i * F, F), F)].astype(f32)
        return a + v * v

    total = lax.fori_loop(0, D // F, square, jnp.zeros((T, F), f32), unroll=4)
    srow = lax.rsqrt(jnp.sum(total.T, axis=0, keepdims=True) / D + 1e-05)
    sc[mine] = srow
    pl.semaphore_wait(bar, NF - 1 + NZ)

    def spread(yy):
        s = slot_of(x, yy, c)
        src = gbuf.at[s]

        @pl.when(jnp.logical_and(yy <= y, y < NY - 1))
        def _():
            to(src, src, gsend.at[yy * 8], grecv.at[s], me + NC, rep).start()

        @pl.when(jnp.logical_and(yy >= y, y > 0))
        def _():
            to(src, src, gsend.at[yy * 8 + 1], grecv.at[s], me - NC, rep).start()
        for j in range(1, NX):
            to(src, src, gsend.at[yy * 8 + 1 + j], grecv.at[s], (x + j) % NX * (NY * NC) + y * NC + c, rep).start()
        to(src, src, gsend.at[yy * 8 + 5], grecv.at[s], me + 1 - 2 * c, rep).start()

    def send_tokens(i, q0, q1):
        def body(k, _):
            dx, dc = shift(k // L)
            d = slot_dev((x + dx) % NX, (y + k) % NY, (c + dc) % NC)
            to(tok.at[:, pl.ds(pl.multiple_of((d * 2 + i) * F, F), F)], tbuf.at[i * NF + mine], tsend.at[i], trecv.at[i * NF + mine], d, rep).start()
            return 0
        lax.fori_loop(max(q0 * L, 1), q1 * L, body, 0)

    def slot_dev(x, y, c):
        return x * (NY * NC) + y * NC + c

    own_g.wait()
    spread(y)

    def send_scale(k, _):
        to(sc.at[mine], sc.at[mine], ssem.at[0], rsem.at[0], (me + k) % NF, rep).start()
        return 0

    lax.fori_loop(1, NF, send_scale, 0)
    send_tokens(0, 0, NX)
    for t in range(1, NY):
        @pl.when(y >= t)
        def _():
            s = slot_of(x, y - t, c)
            wait(gbuf.at[s], grecv.at[s])
            spread(y - t)

        @pl.when(y + t < NY)
        def _():
            s = slot_of(x, y + t, c)
            wait(gbuf.at[s], grecv.at[s])
            spread(y + t)
    send_tokens(0, NX, NG)

    def take_grads(q):
        s0 = base_of(q)

        def body(j, _):
            s = s0 + j
            wait(gbuf.at[s], grecv.at[s])

            @pl.when(q < NX)
            def _():
                to(gbuf.at[s], gbuf.at[s], csend.at[s % (NX * NY)], grecv.at[s], me + 1 - 2 * c, rep).start()
            return 0
        lax.fori_loop(0, L, body, 0)

    def dnormed(q):
        s0 = base_of(q)
        r = lax.dot_general(gbuf[pl.ds(s0, L)].reshape(L * T, C), w[...], (((1,), (1,)), ((), ())), preferred_element_type=f32)
        dn[pl.ds(s0, L)] = r.reshape(L, T, 2 * F)

    def columns(ref):
        flat = jnp.concatenate([ref[s] for s in range(NF)] + [jnp.zeros((T - NF, T), f32)], axis=0).T
        return flat

    def gains(i):
        return gain[pl.ds(me * 2 + i, 1), :]

    def block(i, q):
        s0 = base_of(q)

        def arrive(j, _):
            wait(tbuf.at[i * NF + s0 + j], trecv.at[i * NF + s0 + j])
            return 0
        lax.fori_loop(0, L, arrive, 0)
        v = tbuf[pl.ds(i * NF + s0, L)].astype(f32)
        normed = (v * colc[0, pl.ds(s0, L)] * gains(i)).astype(bf16).reshape(L * T, F)
        part = lax.dot_general(normed, gbuf[pl.ds(s0, L)].reshape(L * T, C), (((0,), (0,)), ((), ())), preferred_element_type=f32)
        acc[i] += part
        return s0, v * gains(i) * dn[pl.ds(s0, L), :, i * F:(i + 1) * F]

    def first(q, _):
        @pl.when(q > 0)
        def _():
            take_grads(q)
        dnormed(q)
        s0, p = block(0, q)
        pacc[pl.ds(s0, L)] = p
        return 0

    acc[...] = jnp.zeros_like(acc)
    wait(sc.at[pl.ds(0, NF - 1)], rsem.at[0])
    flat = columns(sc)
    for s in range(NF):
        colc[0, s] = flat[:, s:s + 1]
    send_tokens(1, 0, NX)
    lax.fori_loop(0, NX, first, 0)
    send_tokens(1, NX, NG)
    lax.fori_loop(NX, NG, first, 0)

    def dw_scatter(i):
        if i:
            accb[...] = acc[i].astype(bf16)
        src, dst = (accb, rsb) if i else (acc.at[0], rsf)
        for p in range(OWN):
            zo = p // 2 * 3 + p % 2

            @pl.when(z != zo)
            def _():
                to(src.at[pl.ds(p * PR, PR)], dst.at[z], ssem.at[3 + i], rsem.at[3 + i], me, zo * NH + h).start()

    def dw_pair(i):
        dst = rsb if i else rsf

        @pl.when(owner)
        def _():
            wait(dst.at[pl.ds(0, NZ - 1)], rsem.at[3 + i])
            own = acc[i, pl.ds(pl.multiple_of(piece * PR, PR), PR)]
            dst[z] = jnp.zeros((PR, C), dst.dtype)
            psum[i] = functools.reduce(jnp.add, [own] + [dst[j].astype(f32) for j in range(NZ)])
            to(psum.at[i], prb.at[i], ssem.at[5 + i], rsem.at[5 + i], me, z * NH + 1 - h).start()

    def dw_gather(i):
        @pl.when(owner)
        def _():
            wait(prb.at[i], rsem.at[5 + i])
            agb[i, piece] = (psum[i] + prb[i]).astype(bf16)

            def body(k, _):
                to(agb.at[i, piece], agb.at[i, piece], ssem.at[7 + i], rsem.at[7 + i], me, (z + k) % NZ * NH + h).start()
                return 0
            lax.fori_loop(1, NZ, body, 0)

    def dw_finish(i):
        @pl.when(owner)
        def _():
            wait(agb.at[i, pl.ds(0, OWN - 1)], rsem.at[7 + i])

        @pl.when(jnp.logical_not(owner))
        def _():
            wait(agb.at[i, pl.ds(0, OWN)], rsem.at[7 + i])
        for p in range(OWN):
            dwb[pl.ds(i * F + p * PR, PR), :] = agb[i, p].astype(f32)
        local(dwb.at[pl.ds(i * F, F)], dw.at[pl.ds(i * F, F)], lsem.at[2 + i]).start()

    def second(q, _):
        s0, p = block(1, q)
        dx, dc = shift(q)
        p = p + pacc[pl.ds(s0, L)]
        for j in range(L):
            rows[0, s0 + j] = jnp.sum(p[j].T, axis=0, keepdims=True)
            d = slot_dev((x + NX - dx) % NX, j, (c + dc) % NC)

            @pl.when(d != me)
            def _():
                to(rows.at[0, s0 + j], rows.at[1, mine], ssem.at[1], rsem.at[1], d, rep).start()
        return 0

    dw_scatter(0)
    lax.fori_loop(0, NG // 2, second, 0)
    dw_pair(0)
    lax.fori_loop(NG // 2, NG * 3 // 4, second, 0)
    dw_gather(0)
    lax.fori_loop(NG * 3 // 4, NG, second, 0)
    dw_scatter(1)

    wait(rows.at[1, pl.ds(0, NF - 1)], rsem.at[1])
    rows[1, mine] = rows[0, mine]
    inner = functools.reduce(jnp.add, [rows[1, s] for s in range(NF)])
    srow = sc[mine]
    rows[2, mine] = srow * srow * srow * inner / D

    def send_coef(k, _):
        to(rows.at[2, mine], rows.at[2, mine], ssem.at[2], rsem.at[2], (me + k) % NF, rep).start()
        return 0

    lax.fori_loop(1, NF, send_coef, 0)
    dw_finish(0)
    dw_pair(1)
    wait(rows.at[2, pl.ds(0, NF - 1)], rsem.at[2])
    flat = columns(rows.at[2])
    for s in range(NF):
        colc[1, s] = flat[:, s:s + 1]

    def finish(k, _):
        xs = k // (NY * NC)
        s = slot_of(xs, (k // NC) % NY, k % NC)
        for i in range(2):
            a = colc[0, s] * gains(i) * dn[s, :, i * F:(i + 1) * F]
            dtb[k, :, i * F:(i + 1) * F] = (a - tbuf[i * NF + s].astype(f32) * colc[1, s]).astype(bf16)
        local(dtb.at[k], dt.at[pl.ds(pl.multiple_of(k * T, T), T)], lsem.at[4]).start()
        return 0

    lax.fori_loop(0, NF, finish, 0)
    dw_gather(1)
    dw_finish(1)

    for i in range(2):
        wait(tbuf.at[pl.ds(0, NF - 1)], tsend.at[i])
        wait(dwb.at[pl.ds(i * F, F)], lsem.at[2 + i])

        @pl.when(owner)
        def _():
            wait((accb if i else acc.at[0]).at[pl.ds(0, F - PR)], ssem.at[3 + i])
            wait(psum.at[i], ssem.at[5 + i])
            wait(agb.at[pl.ds(0, 1)].at[0, pl.ds(0, OWN)], ssem.at[7 + i])
            wait(agb.at[0, pl.ds(0, NZ - 1 - OWN)], ssem.at[7 + i])

        @pl.when(jnp.logical_not(owner))
        def _():
            wait(accb if i else acc.at[0], ssem.at[3 + i])
    for i in range(3):
        wait(rows.at[0, pl.ds(0, NF - 1)], ssem.at[i])
    for yy in range(NY):
        @pl.when(jnp.logical_and(yy <= y, y < NY - 1))
        def _():
            wait(gbuf.at[0], gsend.at[yy * 8])

        @pl.when(jnp.logical_and(yy >= y, y > 0))
        def _():
            wait(gbuf.at[0], gsend.at[yy * 8 + 1])
        for j in range(2, 6):
            wait(gbuf.at[0], gsend.at[yy * 8 + j])
    for q in range(1, NX):
        for j in range(L):
            wait(gbuf.at[0], csend.at[base_of(q) % (NX * NY) + j])
    wait(dtb, lsem.at[4])


def body(tokens, norm_gain, w_value, grad_value):
    hbm, anyspace, vmem = pl.BlockSpec(memory_space=pltpu.HBM), pl.BlockSpec(memory_space=pl.ANY), pl.BlockSpec(memory_space=pltpu.VMEM)
    dma = pltpu.SemaphoreType.DMA
    dw, dt = pl.pallas_call(
        kernel,
        out_shape=(jax.ShapeDtypeStruct((2 * F, C), f32), jax.ShapeDtypeStruct((NF * T, 2 * F), bf16)),
        in_specs=[hbm, vmem, vmem, hbm],
        out_specs=(anyspace, anyspace),
        scratch_shapes=[
            pltpu.VMEM((T, D), bf16),
            pltpu.VMEM((2 * NF, T, F), bf16),
            pltpu.VMEM((NF, T, C), bf16),
            pltpu.VMEM((NF, T, 2 * F), f32),
            pltpu.VMEM((NF, T, F), f32),
            pltpu.VMEM((NF, 1, T), f32),
            pltpu.VMEM((2, NF, T, 1), f32),
            pltpu.VMEM((3, NF, 1, T), f32),
            pltpu.VMEM((2, F, C), f32),
            pltpu.VMEM((F, C), bf16),
            pltpu.VMEM((NZ, PR, C), f32),
            pltpu.VMEM((NZ, PR, C), bf16),
            pltpu.VMEM((2, PR, C), f32),
            pltpu.VMEM((2, PR, C), f32),
            pltpu.VMEM((2, OWN, PR, C), bf16),
            pltpu.VMEM((NF, T, 2 * F), bf16),
            pltpu.VMEM((2 * F, C), f32),
            dma((5,)), dma((NY * 8,)), dma((NX * NY,)), dma((NF,)), dma((2,)), dma((2 * NF,)), dma((9,)), dma((9,)),
        ],
        compiler_params=pltpu.CompilerParams(collective_id=0, has_side_effects=True, vmem_limit_bytes=48 << 20),
    )(tokens.reshape(T, D), norm_gain.reshape(2 * NF, F), w_value, grad_value.reshape(T, C))
    return dw, dt.reshape(NF * T, 1, 2 * F)


def solution(mesh):
    assert mesh.shape["fsdp"] == NF and mesh.shape["rep"] == NR
    in_specs = (P("fsdp", "rep", None), P(), P("fsdp", None), P("fsdp", "rep", None))
    out_specs = (P("fsdp", None), P(None, "rep", "fsdp"))
    return jax.shard_map(body, mesh=mesh, in_specs=in_specs, out_specs=out_specs, check_vma=False)
```

time: 140 us -> 117 us (0.84)
  the two profiles are of different devices: /device:TPU:14 before, /device:TPU:2 now
where the time goes in v2:
time: 117 us
  Pallas kernels  110 us (94%)
  local copies, waits for them, and re-layouts  6.31 us (5%)
    pallas_call x1, Pallas kernels, body(): pl.pallas_call(kernel, out_shape=(jax.ShapeDtypeStruct((2 * F, C), f32),...  110 us
    unnamed x10, local copies, waits for them, and re-layouts  6.31 us

profile of v2, /device:TPU:2, one launch (start us, length us, event | category | flops | bytes accessed | tf_op | source)
XLA Modules:
  0.0 117.2 jit_solution(15133497548015719103)
XLA Ops:
  0.6 0.0 copy-start
  0.6 1.6 %copy-done = bf16[128,1,8192]{2,0,1:T(8,128)(2,1)S(1)} copy-done((bf16[128,1,8192]{2,0,1:T(8,128)(2,1)S(1)}, bf16[128,1,8192]{2,0,1:T(8,128)(2,1)}, u32[]{:S(2)}) %copy-start) | copy-done | bytes 2097176
  2.2 0.0 copy-start.1
  2.2 0.9 copy-done.1
  3.2 0.0 copy-start.2
  3.2 0.9 copy-done.2
  4.1 0.0 copy-start.3
  4.1 0.8 copy-done.3
  4.8 110.3 %shard_map.59 = (f32[256,512]{1,0:T(8,128)S(1)}, bf16[4096,256]{1,0:T(8,128)(2,1)S(1)}) custom-call(bf16[128,8192]{1,0:T(8,128)(2,1)S(1)} %bitcast.4, f32[64,128]{1,0:T(8,128)S(1)} %bitcast.7, bf16[256,512]{1,0:T(8,128)(2,1)S(1)} %copy-done.1, bf16[128,512]{1,0:T(8,128)(2,1)S(1)} %bitcast.6), custom_call_target="tpu_custom_call" | custom-call | tf_op jit(solution)/shard_map/pallas_call | solution.py:324
  115.1 0.8 copy.8
  115.9 1.3 %copy.9 = bf16[4096,1,256]{2,0,1:T(8,128)(2,1)} copy(bf16[4096,1,256]{2,0,1:T(8,128)(2,1)S(1)} %bitcast.5) | data formatting | bytes 4194304
Async XLA Ops:
  0.6 1.6 %copy-start = (bf16[128,1,8192]{2,0,1:T(8,128)(2,1)S(1)}, bf16[128,1,8192]{2,0,1:T(8,128)(2,1)}, u32[]{:S(2)}) copy-start(bf16[128,1,8192]{2,0,1:T(8,128)(2,1)} %param.4) | copy-start | bytes 6291460
  2.2 0.9 copy-start.1
  3.2 0.9 copy-start.2
  4.1 0.8 copy-start.3

commit v3 on v2

--- a/solution.py
+++ b/solution.py
@@ -248,11 +248,8 @@
         return 0
 
     dw_scatter(0)
-    lax.fori_loop(0, NG // 2, second, 0)
+    lax.fori_loop(0, NG, second, 0)
     dw_pair(0)
-    lax.fori_loop(NG // 2, NG * 3 // 4, second, 0)
-    dw_gather(0)
-    lax.fori_loop(NG * 3 // 4, NG, second, 0)
     dw_scatter(1)
 
     wait(rows.at[1, pl.ds(0, NF - 1)], rsem.at[1])
@@ -266,12 +263,14 @@
         return 0
 
     lax.fori_loop(1, NF, send_coef, 0)
-    dw_finish(0)
+    dw_gather(0)
     dw_pair(1)
     wait(rows.at[2, pl.ds(0, NF - 1)], rsem.at[2])
     flat = columns(rows.at[2])
     for s in range(NF):
         colc[1, s] = flat[:, s:s + 1]
+
+    dw_gather(1)
 
     def finish(k, _):
         xs = k // (NY * NC)
@@ -283,7 +282,7 @@
         return 0
 
     lax.fori_loop(0, NF, finish, 0)
-    dw_gather(1)
+    dw_finish(0)
     dw_finish(1)
 
     for i in range(2):
@@ -346,7 +345,7 @@
             pltpu.VMEM((2 * F, C), f32),
             dma((5,)), dma((NY * 8,)), dma((NX * NY,)), dma((NF,)), dma((2,)), dma((2 * NF,)), dma((9,)), dma((9,)),
         ],
-        compiler_params=pltpu.CompilerParams(collective_id=0, has_side_effects=True, vmem_limit_bytes=48 << 20),
+        compiler_params=pltpu.CompilerParams(collective_id=0, has_side_effects=True, vmem_limit_bytes=59 << 20),
     )(tokens.reshape(T, D), norm_gain.reshape(2 * NF, F), w_value, grad_value.reshape(T, C))
     return dw, dt.reshape(NF * T, 1, 2 * F)
 

time: 117 us -> 106 us (0.906)
  the two profiles are of different devices: /device:TPU:2 before, /device:TPU:64 now
where the time goes in v3:
time: 106 us; the launch traced here: 105 us
  Pallas kernels  99.9 us (94%)
  local copies, waits for them, and re-layouts  4.91 us (5%)
    pallas_call x1, Pallas kernels, body(): pl.pallas_call(kernel, out_shape=(jax.ShapeDtypeStruct((2 * F, C), f32),...  99.9 us
    unnamed x2, local copies, waits for them, and re-layouts  4.91 us

profile of v3, /device:TPU:64, one launch (start us, length us, event | category | flops | bytes accessed | tf_op | source)
XLA Modules:
  0.0 105.4 jit_solution(15059831250724101791)
XLA Ops:
  0.6 99.9 %shard_map.59 = (f32[256,512]{1,0:T(8,128)}, bf16[4096,256]{1,0:T(8,128)(2,1)}) custom-call(bf16[128,8192]{1,0:T(8,128)(2,1)} %bitcast.4, f32[64,128]{1,0:T(8,128)} %bitcast.7, bf16[256,512]{1,0:T(8,128)(2,1)} %w.1, bf16[128,512]{1,0:T(8,128)(2,1)} %bitcast.6), custom_call_target="tpu_custom_call" | custom-call | tf_op jit(solution)/shard_map/pallas_call | solution.py:323
  100.5 1.9 %copy.8 = f32[256,512]{1,0:T(8,128)} copy(f32[256,512]{1,0:T(8,128)} %get-tuple-element.8) | data formatting | bytes 1048576
  102.4 3.0 %copy.9 = bf16[4096,1,256]{2,0,1:T(8,128)(2,1)} copy(bf16[4096,1,256]{2,0,1:T(8,128)(2,1)} %bitcast.5) | data formatting | bytes 4194304

commit v4 on v3

--- a/solution.py
+++ b/solution.py
@@ -21,7 +21,7 @@
 f32, bf16 = jnp.float32, jnp.bfloat16
 
 
-def kernel(tok, gain, w, grd, dw, dt, vtok, tbuf, gbuf, dn, pacc, sc, colc, rows, acc, accb, rsf, rsb, psum, prb, agb, dtb, dwb,
+def kernel(tok, gain_in, w_in, grd, dw, dt, vtok, tbuf, gbuf, dn, pacc, sc, colc, rows, acc, accb, rsb, psum, prb, agb, dtb, dwb, gain, w,
            lsem, gsend, csend, grecv, tsend, trecv, ssem, rsem):
     me, rep = lax.axis_index("fsdp"), lax.axis_index("rep")
     x, y, c = me // (NY * NC), (me // NC) % NY, me % NC
@@ -69,18 +69,12 @@
     load.start()
     own_g = local(grd, gbuf.at[mine], lsem.at[1])
     own_g.start()
+    extra = [local(gain_in, gain, lsem.at[5]), local(w_in, w, lsem.at[6])]
+    for cp in extra:
+        cp.start()
     own_t = [local(tok.at[:, pl.ds(pl.multiple_of((me * 2 + i) * F, F), F)], tbuf.at[i * NF + mine], trecv.at[i * NF + mine]) for i in range(2)]
     for cp in own_t:
         cp.start()
-    load.wait()
-
-    def square(i, a):
-        v = vtok[:, pl.ds(pl.multiple_of(i * F, F), F)].astype(f32)
-        return a + v * v
-
-    total = lax.fori_loop(0, D // F, square, jnp.zeros((T, F), f32), unroll=4)
-    srow = lax.rsqrt(jnp.sum(total.T, axis=0, keepdims=True) / D + 1e-05)
-    sc[mine] = srow
     pl.semaphore_wait(bar, NF - 1 + NZ)
 
     def spread(yy):
@@ -111,13 +105,22 @@
 
     own_g.wait()
     spread(y)
+    send_tokens(0, 0, NX)
+    load.wait()
+
+    def square(i, a):
+        v = vtok[:, pl.ds(pl.multiple_of(i * F, F), F)].astype(f32)
+        return a + v * v
+
+    total = lax.fori_loop(0, D // F, square, jnp.zeros((T, F), f32), unroll=4)
+    srow = lax.rsqrt(jnp.sum(total.T, axis=0, keepdims=True) / D + 1e-05)
+    sc[mine] = srow
 
     def send_scale(k, _):
         to(sc.at[mine], sc.at[mine], ssem.at[0], rsem.at[0], (me + k) % NF, rep).start()
         return 0
 
     lax.fori_loop(1, NF, send_scale, 0)
-    send_tokens(0, 0, NX)
     for t in range(1, NY):
         @pl.when(y >= t)
         def _():
@@ -179,6 +182,8 @@
         pacc[pl.ds(s0, L)] = p
         return 0
 
+    for cp in extra:
+        cp.wait()
     acc[...] = jnp.zeros_like(acc)
     wait(sc.at[pl.ds(0, NF - 1)], rsem.at[0])
     flat = columns(sc)
@@ -190,9 +195,8 @@
     lax.fori_loop(NX, NG, first, 0)
 
     def dw_scatter(i):
-        if i:
-            accb[...] = acc[i].astype(bf16)
-        src, dst = (accb, rsb) if i else (acc.at[0], rsf)
+        accb[i] = acc[i].astype(bf16)
+        src, dst = accb.at[i], rsb.at[i]
         for p in range(OWN):
             zo = p // 2 * 3 + p % 2
 
@@ -201,7 +205,7 @@
                 to(src.at[pl.ds(p * PR, PR)], dst.at[z], ssem.at[3 + i], rsem.at[3 + i], me, zo * NH + h).start()
 
     def dw_pair(i):
-        dst = rsb if i else rsf
+        dst = rsb.at[i]
 
         @pl.when(owner)
         def _():
@@ -238,6 +242,9 @@
         s0, p = block(1, q)
         dx, dc = shift(q)
         p = p + pacc[pl.ds(s0, L)]
+        for i in range(2):
+            cols = slice(i * F, (i + 1) * F)
+            dn[pl.ds(s0, L), :, cols] = colc[0, pl.ds(s0, L)] * gains(i) * dn[pl.ds(s0, L), :, cols]
         for j in range(L):
             rows[0, s0 + j] = jnp.sum(p[j].T, axis=0, keepdims=True)
             d = slot_dev((x + NX - dx) % NX, j, (c + dc) % NC)
@@ -248,8 +255,9 @@
         return 0
 
     dw_scatter(0)
-    lax.fori_loop(0, NG, second, 0)
+    lax.fori_loop(0, NG - 1, second, 0)
     dw_pair(0)
+    lax.fori_loop(NG - 1, NG, second, 0)
     dw_scatter(1)
 
     wait(rows.at[1, pl.ds(0, NF - 1)], rsem.at[1])
@@ -275,9 +283,9 @@
     def finish(k, _):
         xs = k // (NY * NC)
         s = slot_of(xs, (k // NC) % NY, k % NC)
+        coef = colc[1, s]
         for i in range(2):
-            a = colc[0, s] * gains(i) * dn[s, :, i * F:(i + 1) * F]
-            dtb[k, :, i * F:(i + 1) * F] = (a - tbuf[i * NF + s].astype(f32) * colc[1, s]).astype(bf16)
+            dtb[k, :, i * F:(i + 1) * F] = (dn[s, :, i * F:(i + 1) * F] - tbuf[i * NF + s].astype(f32) * coef).astype(bf16)
         local(dtb.at[k], dt.at[pl.ds(pl.multiple_of(k * T, T), T)], lsem.at[4]).start()
         return 0
 
@@ -291,14 +299,14 @@
 
         @pl.when(owner)
         def _():
-            wait((accb if i else acc.at[0]).at[pl.ds(0, F - PR)], ssem.at[3 + i])
+            wait(accb.at[i, pl.ds(0, F - PR)], ssem.at[3 + i])
             wait(psum.at[i], ssem.at[5 + i])
             wait(agb.at[pl.ds(0, 1)].at[0, pl.ds(0, OWN)], ssem.at[7 + i])
             wait(agb.at[0, pl.ds(0, NZ - 1 - OWN)], ssem.at[7 + i])
 
         @pl.when(jnp.logical_not(owner))
         def _():
-            wait(accb if i else acc.at[0], ssem.at[3 + i])
+            wait(accb.at[i], ssem.at[3 + i])
     for i in range(3):
         wait(rows.at[0, pl.ds(0, NF - 1)], ssem.at[i])
     for yy in range(NY):
@@ -318,12 +326,12 @@
 
 
 def body(tokens, norm_gain, w_value, grad_value):
-    hbm, anyspace, vmem = pl.BlockSpec(memory_space=pltpu.HBM), pl.BlockSpec(memory_space=pl.ANY), pl.BlockSpec(memory_space=pltpu.VMEM)
+    hbm, anyspace = pl.BlockSpec(memory_space=pltpu.HBM), pl.BlockSpec(memory_space=pl.ANY)
     dma = pltpu.SemaphoreType.DMA
     dw, dt = pl.pallas_call(
         kernel,
         out_shape=(jax.ShapeDtypeStruct((2 * F, C), f32), jax.ShapeDtypeStruct((NF * T, 2 * F), bf16)),
-        in_specs=[hbm, vmem, vmem, hbm],
+        in_specs=[hbm] * 4,
         out_specs=(anyspace, anyspace),
         scratch_shapes=[
             pltpu.VMEM((T, D), bf16),
@@ -335,15 +343,16 @@
             pltpu.VMEM((2, NF, T, 1), f32),
             pltpu.VMEM((3, NF, 1, T), f32),
             pltpu.VMEM((2, F, C), f32),
-            pltpu.VMEM((F, C), bf16),
-            pltpu.VMEM((NZ, PR, C), f32),
-            pltpu.VMEM((NZ, PR, C), bf16),
+            pltpu.VMEM((2, F, C), bf16),
+            pltpu.VMEM((2, NZ, PR, C), bf16),
             pltpu.VMEM((2, PR, C), f32),
             pltpu.VMEM((2, PR, C), f32),
             pltpu.VMEM((2, OWN, PR, C), bf16),
             pltpu.VMEM((NF, T, 2 * F), bf16),
             pltpu.VMEM((2 * F, C), f32),
-            dma((5,)), dma((NY * 8,)), dma((NX * NY,)), dma((NF,)), dma((2,)), dma((2 * NF,)), dma((9,)), dma((9,)),
+            pltpu.VMEM((2 * NF, F), f32),
+            pltpu.VMEM((2 * F, C), bf16),
+            dma((7,)), dma((NY * 8,)), dma((NX * NY,)), dma((NF,)), dma((2,)), dma((2 * NF,)), dma((9,)), dma((9,)),
         ],
         compiler_params=pltpu.CompilerParams(collective_id=0, has_side_effects=True, vmem_limit_bytes=59 << 20),
     )(tokens.reshape(T, D), norm_gain.reshape(2 * NF, F), w_value, grad_value.reshape(T, C))

time: 106 us -> 103 us (0.972)
  the two profiles are of different devices: /device:TPU:64 before, /device:TPU:25 now
where the time goes in v4:
time: 103 us
  Pallas kernels  97.3 us (94%)
  local copies, waits for them, and re-layouts  4.91 us (5%)
    pallas_call x1, Pallas kernels, body(): pl.pallas_call(kernel, out_shape=(jax.ShapeDtypeStruct((2 * F, C), f32),...  97.3 us
    unnamed x2, local copies, waits for them, and re-layouts  4.91 us

profile of v4, /device:TPU:25, one launch (start us, length us, event | category | flops | bytes accessed | tf_op | source)
XLA Modules:
  0.0 102.9 jit_solution(14291477216522119018)
XLA Ops:
  0.6 97.3 %shard_map.59 = (f32[256,512]{1,0:T(8,128)}, bf16[4096,256]{1,0:T(8,128)(2,1)}) custom-call(bf16[128,8192]{1,0:T(8,128)(2,1)} %bitcast.4, f32[64,128]{1,0:T(8,128)} %bitcast.7, bf16[256,512]{1,0:T(8,128)(2,1)} %w_in.1, bf16[128,512]{1,0:T(8,128)(2,1)} %bitcast.6), custom_call_target="tpu_custom_call" | custom-call | tf_op jit(solution)/shard_map/pallas_call | solution.py:331
  97.9 1.9 %copy.8 = f32[256,512]{1,0:T(8,128)} copy(f32[256,512]{1,0:T(8,128)} %get-tuple-element.8) | data formatting | bytes 1048576
  99.8 3.0 %copy.9 = bf16[4096,1,256]{2,0,1:T(8,128)(2,1)} copy(bf16[4096,1,256]{2,0,1:T(8,128)(2,1)} %bitcast.5) | data formatting | bytes 4194304
